TPU v7x, 32 devices: a whole 2x2x4 slice. The times are simulated.
32 devices in a mesh: sec: 2 (over y), tube: 4 (over z), blk: 2 (over x), sub: 2 (over core).
Axes of the slice: x: 2, y: 2, z: 4, core: 2. Of those that a mesh axis runs over, the one named last changes fastest.
Arguments:
- latent: float32 [2048, 256], P(('sec', 'tube'), 'blk'), parts along dimension 0, may hold values from 0.2 to 5
- weight_maps: bfloat16 [8, 2048, 256], P('sub', ('sec', 'tube'), 'blk'), parts along dimension 1, may hold values from 0.039794922 to 0.19921875
- row_taps: float32 [8, 31], P('sub'), may hold values from 0.05 to 1
- col_taps: float32 [8, 31], P('sub'), may hold values from 0.05 to 1
- exposures: bfloat16 [2, 512, 128, 128], P('blk', ('sec', 'tube')), parts along dimension 1, may hold values from 0.19921875 to 5
- gains: bfloat16 [2, 512], P('blk', ('sec', 'tube')), parts along dimension 1, may hold values from 0.5 to 2
- owners: int32 [2, 512, 1], P('blk', ('sec', 'tube')), parts along dimension 1, may hold values from 0 to 3, as said below
- offsets: int32 [2, 512], P('blk', ('sec', 'tube')), parts along dimension 1, may hold values from 0 to 1, as said below
Outputs:
- updated: float32 [2048, 256], P(('sec', 'tube'), 'blk'), parts along dimension 0
There are 2 independent parts, one for each index of `sec`. A program takes and returns all parts, laid end to end along the dimension named above; an argument that names none is the same for every part. Nothing has to cross between parts.
Inputs may be any that keep to these rules, and one draw needn't show every extreme that they name: `owners`: among the 64 slots of one device no tube position is named more than 32 times; in each column of blocks some tube position is named exactly 32 times by every device of that column. `offsets`: some block places of the image receive no slot.
All inputs are finite; a program needn't handle non-finite values.
Results may differ from a plain program's by a relative error of at most 0.00035.
Values may be sent and summed in bfloat16 or wider, within the bound.
A program may use at most 64 MiB of HBM per device.

v0:
```python
import jax
import jax.numpy as jnp
from jax import lax
from jax.sharding import PartitionSpec as P


def extended(block, sides, width, periodic):
    for axis, dim in sides:
        count = lax.axis_size(axis)
        forward = [(i, i + 1) for i in range(count - 1)]
        if periodic:
            forward.append((count - 1, 0))
        backward = [(target, source) for source, target in forward]
        low = lax.ppermute(
            lax.slice_in_dim(block, block.shape[dim] - width, None, axis=dim), axis, forward
        )
        high = lax.ppermute(lax.slice_in_dim(block, 0, width, axis=dim), axis, backward)
        block = jnp.concatenate([low, block, high], axis=dim)
    return block


def sweep(source, tap_stack, length, dimension):
    running = tap_stack[0] * lax.slice_in_dim(source, 0, length, axis=dimension)
    for tap_index in range(1, tap_stack.shape[0]):
        running = running + tap_stack[tap_index] * lax.slice_in_dim(
            source, tap_index, tap_index + length, axis=dimension
        )
    return running


def separable(source, row_stack, col_stack, out_rows, out_cols):
    row_pass = sweep(source, row_stack, out_rows, source.ndim - 2)
    return sweep(row_pass, col_stack, out_cols, row_pass.ndim - 1)


def body(latent, weight_maps, row_taps, col_taps, exposures, gains, owners, offsets):
    tile_rows, block_size = latent.shape
    tap_count = row_taps.shape[1]
    margin = tap_count // 2
    row_blocks = tile_rows // block_size
    slot_count = exposures.shape[1]
    tube_count = lax.axis_size("tube")
    capacity = max(2, 2 * slot_count // tube_count)
    row_norm = row_taps / jnp.sum(row_taps, axis=1, keepdims=True)
    col_norm = col_taps / jnp.sum(col_taps, axis=1, keepdims=True)
    row_ahead = row_norm.T[:, :, None, None]
    col_ahead = col_norm.T[:, :, None, None]
    row_behind = row_norm[:, ::-1].T[:, :, None, None]
    col_behind = col_norm[:, ::-1].T[:, :, None, None]
    weight_stack = weight_maps.astype(jnp.float32)
    target = owners[0, :, 0]
    placement_plan = (offsets[0][:, None] == jnp.arange(row_blocks)[None, :]).astype(jnp.bfloat16)
    earlier = jnp.arange(slot_count)[None, :] < jnp.arange(slot_count)[:, None]
    matching = target[:, None] == target[None, :]
    order_rank = jnp.sum(matching & earlier, axis=1)
    picked_tube = (target[None, None, :] == jnp.arange(tube_count)[:, None, None]) & (
        order_rank[None, None, :] == jnp.arange(capacity)[None, :, None]
    )
    picked_tube = picked_tube.astype(jnp.bfloat16)
    send_blocks = jnp.einsum(
        "mew,wng->meng", picked_tube, exposures[0], preferred_element_type=jnp.float32
    ).astype(jnp.bfloat16)
    send_places = jnp.einsum(
        "jaf,fu->jau", picked_tube, placement_plan, preferred_element_type=jnp.float32
    ).astype(jnp.bfloat16)
    send_gains = jnp.einsum(
        "jaf,fu->jau",
        picked_tube,
        placement_plan * gains[0][:, None],
        preferred_element_type=jnp.float32,
    ).astype(jnp.bfloat16)
    got_blocks, received_positions, got_gains = (
        lax.all_to_all(send_blocks, "tube", split_axis=0, concat_axis=0, tiled=True),
        lax.all_to_all(send_places, "tube", split_axis=0, concat_axis=0, tiled=True),
        lax.all_to_all(send_gains, "tube", split_axis=0, concat_axis=0, tiled=True),
    )
    count_blocks = jnp.einsum(
        "tcr,tcxy->rxy", received_positions, got_blocks, preferred_element_type=jnp.float32
    )
    gain_blocks = jnp.sum(got_gains.astype(jnp.float32), axis=(0, 1))
    counts = count_blocks.reshape(tile_rows, block_size)
    coverage = jnp.broadcast_to(
        jnp.repeat(gain_blocks, block_size)[:, None], (tile_rows, block_size)
    )
    padded = extended(latent.astype(jnp.bfloat16), (("tube", 0),), margin, False).astype(
        latent.dtype
    )
    padded = extended(padded.astype(jnp.bfloat16), (("blk", 1),), margin, True).astype(padded.dtype)
    partial_value = jnp.sum(
        weight_stack * separable(padded[None], row_ahead, col_ahead, tile_rows, block_size), axis=0
    )
    smeared_image = lax.psum(partial_value.astype(jnp.bfloat16), "sub").astype(jnp.float32)
    quotient = counts / smeared_image
    stacked = jnp.stack([weight_stack * quotient[None], weight_stack * coverage[None]])
    weighted = extended(stacked, (("tube", 2),), margin, False)
    weighted = extended(weighted, (("blk", 3),), margin, True)
    backward = jnp.sum(separable(weighted, row_behind, col_behind, tile_rows, block_size), axis=1)
    numerator, denominator = lax.psum((backward[0], backward[1]), "sub")
    return latent * numerator / jnp.maximum(denominator, 0.25)


def solution(mesh):
    in_specs = (
        P(("sec", "tube"), "blk"),
        P("sub", ("sec", "tube"), "blk"),
        P("sub", None),
        P("sub", None),
        P("blk", ("sec", "tube"), None, None),
        P("blk", ("sec", "tube")),
        P("blk", ("sec", "tube"), None),
        P("blk", ("sec", "tube")),
    )
    out_specs = P(("sec", "tube"), "blk")
    return jax.shard_map(body, mesh=mesh, in_specs=in_specs, out_specs=out_specs, check_vma=False)
```

profile of v0, /device:TPU:0, one launch (start us, length us, event | category | flops | bytes accessed | tf_op | source)
XLA Modules:
  0.0 301.7 jit_solution(13113632499515899674)
XLA Ops:
  9.6 6.3 %all-to-all-start = ((bf16[4,32,2]{1,2,0:T(2,128)(2,1)}), bf16[4,32,2]{1,2,0:T(2,128)(2,1)S(1)}, u32[]{:S(2)}, u32[]{:S(2)}) async-start(bf16[4,32,2]{1,2,0:T(2,128)(2,1)} %convolution_convert_fusion.2), calls=%async_computation | async-start | bytes 4096 | tf_op jit(solution)/shard_map/all_to_all | solution.py:74
  17.3 4.1 %all-to-all-done = bf16[4,32,2]{1,2,0:T(2,128)(2,1)S(1)} async-done(((bf16[4,32,2]{1,2,0:T(2,128)(2,1)}), bf16[4,32,2]{1,2,0:T(2,128)(2,1)S(1)}, u32[]{:S(2)}, u32[]{:S(2)}) %all-to-all-start) | async-done | bytes 544 | tf_op jit(solution)/shard_map/all_to_all | solution.py:74
  21.4 3.2 %all-to-all-start.2 = ((bf16[4,32,2]{1,2,0:T(2,128)(2,1)}), bf16[4,32,2]{1,2,0:T(2,128)(2,1)S(1)}, u32[]{:S(2)}, u32[]{:S(2)}) async-start(bf16[4,32,2]{1,2,0:T(2,128)(2,1)} %convolution_convert_fusion.1), calls=%async_computation.2 | async-start | bytes 4096 | tf_op jit(solution)/shard_map/all_to_all | solution.py:75
  24.6 1.9 convolution_convert_fusion
  26.5 2.7 copy.88
  30.1 4.8 %all-to-all-start.1 = ((bf16[4,32,128,128]{3,1,2,0:T(8,128)(2,1)}), bf16[4,32,128,128]{3,1,2,0:T(8,128)(2,1)}, u32[]{:S(2)}, u32[]{:S(2)}) async-start(bf16[4,32,128,128]{3,1,2,0:T(8,128)(2,1)} %copy.88), calls=%async_computation.1 | async-start | bytes 8388608 | tf_op jit(solution)/shard_map/all_to_all | solution.py:73
  36.3 4.7 %collective-permute-start = (bf16[15,128]{1,0:T(8,128)(2,1)S(1)}, bf16[15,128]{1,0:T(8,128)(2,1)S(1)}, u32[]{:S(2)}, u32[]{:S(2)}) collective-permute-start(bf16[15,128]{1,0:T(8,128)(2,1)S(1)} %get-tuple-element.174), channel_id=1, source_target_pairs={{0,4},{4,8},{8,12},{1,5},{5,9},{9,13},{2,6},{6,10},{10,14},{3,7},{... | collective-permute-start | bytes 11528 | tf_op jit(solution)/shard_map/ppermute | solution.py:14
  46.6 33.9 %collective-permute-done.1 = bf16[15,128]{1,0:T(8,128)(2,1)S(1)} collective-permute-done((bf16[15,128]{1,0:T(8,128)(2,1)S(1)}, bf16[15,128]{1,0:T(8,128)(2,1)S(1)}, u32[]{:S(2)}, u32[]{:S(2)}) %collective-permute-start.1) | collective-permute-done | bytes 3872 | tf_op jit(solution)/shard_map/ppermute | solution.py:17
  80.6 20.3 %collective-permute-done = bf16[15,128]{1,0:T(8,128)(2,1)S(1)} collective-permute-done((bf16[15,128]{1,0:T(8,128)(2,1)S(1)}, bf16[15,128]{1,0:T(8,128)(2,1)S(1)}, u32[]{:S(2)}, u32[]{:S(2)}) %collective-permute-start) | collective-permute-done | bytes 3872 | tf_op jit(solution)/shard_map/ppermute | solution.py:14
  107.0 2.1 slice_bitcast_fusion.30
  109.1 1.7 copy.121
  110.9 1.7 copy.120
  112.6 1.7 copy.119
  114.3 1.7 copy.118
  116.0 1.7 copy.117
  117.7 1.7 copy.116
  119.4 1.7 copy.115
  121.2 1.7 copy.114
  122.9 1.7 copy.113
  124.6 1.7 copy.112
  126.3 1.7 copy.111
  128.0 1.7 copy.110
  129.8 1.7 copy.109
  131.5 1.7 copy.108
  133.2 1.7 copy.107
  134.9 1.7 copy.106
  139.8 1.7 copy.103
  141.5 1.7 copy.102
  143.3 1.7 copy.101
  145.0 1.8 copy.100
  146.7 1.7 copy.99
  148.5 1.7 copy.98
  150.2 1.7 copy.97
  151.9 1.7 copy.96
  153.6 1.7 copy.95
  157.4 10.0 %multiply_add_fusion = f32[4,256,158]{1,0,2:T(4,128)S(1)} fusion(f32[256,158]{0,1:T(8,128)S(1)} %copy-done.2, f32[4]{0:T(128)} %get-tuple-element.99, f32[256,158]{0,1:T(8,128)} %copy.120, f32[4]{0:T(128)} %get-tuple-element.100, f32[256,158]{0,1:T(8,128)} %copy.119, f32[4]{0:T(128)} %get-tuple-element.101, f32[256,158]{0,1:T(8,128)} %copy.118, ...), kind=kLoop, calls=%fused_computation.134 | loop fusion | flops 9869312 | bytes 5663216 | tf_op jit(solution)/shard_map/add | solution.py:25
  167.7 4.4 %fusion.62 = bf16[256,128]{0,1:T(8,128)(2,1)} fusion(bf16[4,256,128]{1,0,2:T(4,128)(2,1)S(1)} %copy.86, f32[4,256,158]{1,0,2:T(4,128)S(1)} %multiply_add_fusion, f32[4]{0:T(128)S(1)} %copy-done.15, f32[4]{0:T(128)S(1)} %copy-done.16, f32[4]{0:T(128)S(1)} %copy-done.17, f32[4]{0:T(128)S(1)} %copy-done.18, f32[4]{0:T(128)S(1)} %copy-done.19, ...), kind=kLoop, calls=%fused_computation.135 | loop fusion | flops 8355840 | bytes 16581104 | tf_op jit(solution)/shard_map/reduce_sum | solution.py:89
  172.3 2.9 convolution_bitcast_fusion
  175.3 37.7 %all-reduce.4.cloned.1.call-done = bf16[256,128]{0,1:T(8,128)(2,1)} async-done(((bf16[256,128]{0,1:T(8,128)(2,1)}), bf16[256,128]{0,1:T(8,128)(2,1)}) %all-reduce.4.cloned.1.call-update) | async-done | bytes 65552 | tf_op jit(solution)/shard_map/psum | solution.py:92
  215.8 4.8 %collective-permute-start.4 = (f32[2,4,15,128]{2,1,3,0:T(4,128)S(1)}, f32[2,4,15,128]{2,1,3,0:T(4,128)S(1)}, u32[]{:S(2)}, u32[]{:S(2)}) collective-permute-start(f32[2,4,15,128]{2,1,3,0:T(4,128)S(1)} %get-tuple-element.133), channel_id=1, source_target_pairs={{0,4},{4,8},{8,12},{1,5},{5,9},{9,13},{2,6},{6,10},{10,14},{3,7},{... | collective-permute-start | bytes 184328 | tf_op jit(solution)/shard_map/ppermute | solution.py:14
  221.0 9.6 %collective-permute-done.5 = f32[2,4,15,128]{2,1,3,0:T(4,128)S(1)} collective-permute-done((f32[2,4,15,128]{2,1,3,0:T(4,128)S(1)}, f32[2,4,15,128]{2,1,3,0:T(4,128)S(1)}, u32[]{:S(2)}, u32[]{:S(2)}) %collective-permute-start.5) | collective-permute-done | bytes 61472 | tf_op jit(solution)/shard_map/ppermute | solution.py:17
  232.0 1.8 collective-permute-start.7
  235.0 4.7 %collective-permute-done.7 = f32[2,4,286,15]{2,1,3,0:T(4,128)S(1)} collective-permute-done((f32[2,4,286,15]{2,1,3,0:T(4,128)S(1)}, f32[2,4,286,15]{2,1,3,0:T(4,128)S(1)}, u32[]{:S(2)}, u32[]{:S(2)}) %collective-permute-start.7) | collective-permute-done | bytes 137312 | tf_op jit(solution)/shard_map/ppermute | solution.py:17
  239.7 2.1 collective-permute-done.6
  241.8 2.6 pad_maximum_fusion
  244.3 20.9 %fusion.1 = f32[2,4,256,158]{2,1,3,0:T(4,128)S(1)} fusion(f32[2,4,286,158]{2,1,3,0:T(4,128)S(1)} %pad_maximum_fusion, f32[4]{0:T(128)S(1)} %get-tuple-element.37, f32[4]{0:T(128)S(1)} %get-tuple-element.38, f32[4]{0:T(128)S(1)} %get-tuple-element.39, f32[4]{0:T(128)S(1)} %get-tuple-element.40, f32[4]{0:T(128)S(1)} %get-tuple-element.41, ...), kind=kLoop, calls=%fused_computation.4 | loop fusion | flops 19738624 | bytes 41419248 | tf_op jit(solution)/shard_map/add | solution.py:25
  265.2 6.5 %fusion.32 = f32[2,256,128]{1,2,0:T(8,128)S(1)} fusion(f32[2,4,256,158]{2,1,3,0:T(4,128)S(1)} %fusion.1, f32[4]{0:T(128)S(1)} %get-tuple-element.6, f32[4]{0:T(128)S(1)} %get-tuple-element.7, f32[4]{0:T(128)S(1)} %get-tuple-element.8, f32[4]{0:T(128)S(1)} %get-tuple-element.9, f32[4]{0:T(128)S(1)} %get-tuple-element.10, f32[4]{0:T(128)S(1)} %get-tuple-element.11, ...), kind=kLoop, calls=%fused_computation.69 | loop fusion | flops 16187392 | bytes 32768496 | tf_op jit(solution)/shard_map/reduce_sum | solution.py:97
  272.6 20.5 %all-reduce.6.cloned.1.call-done = (f32[256,128]{0,1:T(8,128)}, f32[256,128]{0,1:T(8,128)}) async-done(((f32[256,128]{0,1:T(8,128)}, f32[256,128]{0,1:T(8,128)}), (f32[256,128]{0,1:T(8,128)}, f32[256,128]{0,1:T(8,128)})) %all-reduce.6.cloned.1.call-update) | async-done | bytes 262160 | tf_op jit(solution)/shard_map/psum | solution.py:98
  (128 shorter events, 31.9 us)
Async XLA Ops:
  6.5 18.1 %copy-start = (bf16[1,64,128,128]{3,2,1,0:T(8,128)(2,1)S(1)}, bf16[1,64,128,128]{3,2,1,0:T(8,128)(2,1)}, u32[]{:S(2)}) copy-start(bf16[1,64,128,128]{3,2,1,0:T(8,128)(2,1)} %param.12) | copy-start | bytes 6291460
  9.6 11.8 %all-to-all-start = ((bf16[4,32,2]{1,2,0:T(2,128)(2,1)}), bf16[4,32,2]{1,2,0:T(2,128)(2,1)S(1)}, u32[]{:S(2)}, u32[]{:S(2)}) async-start(bf16[4,32,2]{1,2,0:T(2,128)(2,1)} %convolution_convert_fusion.2), calls=%async_computation | async-start | bytes 4096 | tf_op jit(solution)/shard_map/all_to_all | solution.py:74
  21.4 8.7 %all-to-all-start.2 = ((bf16[4,32,2]{1,2,0:T(2,128)(2,1)}), bf16[4,32,2]{1,2,0:T(2,128)(2,1)S(1)}, u32[]{:S(2)}, u32[]{:S(2)}) async-start(bf16[4,32,2]{1,2,0:T(2,128)(2,1)} %convolution_convert_fusion.1), calls=%async_computation.2 | async-start | bytes 4096 | tf_op jit(solution)/shard_map/all_to_all | solution.py:75
  29.3 5.7 %copy-start.3 = (f32[256,128]{1,0:T(8,128)S(1)}, f32[256,128]{1,0:T(8,128)}, u32[]{:S(2)}) copy-start(f32[256,128]{1,0:T(8,128)} %param.8) | copy-start | bytes 393220
  29.3 11.8 %copy-start.5 = (bf16[4,256,128]{2,1,0:T(8,128)(2,1)S(1)}, bf16[4,256,128]{2,1,0:T(8,128)(2,1)}, u32[]{:S(2)}) copy-start(bf16[4,256,128]{2,1,0:T(8,128)(2,1)} %param.9) | copy-start | bytes 786436
  29.3 12.0 %copy-start.6 = (f32[4,31]{1,0:T(4,128)S(1)}, f32[4,31]{1,0:T(4,128)}, u32[]{:S(2)}) copy-start(f32[4,31]{1,0:T(4,128)} %param.10) | copy-start | bytes 1492
  29.3 12.1 %copy-start.7 = (f32[4,31]{1,0:T(4,128)S(1)}, f32[4,31]{1,0:T(4,128)}, u32[]{:S(2)}) copy-start(f32[4,31]{1,0:T(4,128)} %param.11) | copy-start | bytes 1492
  30.1 142.2 %all-to-all-start.1 = ((bf16[4,32,128,128]{3,1,2,0:T(8,128)(2,1)}), bf16[4,32,128,128]{3,1,2,0:T(8,128)(2,1)}, u32[]{:S(2)}, u32[]{:S(2)}) async-start(bf16[4,32,128,128]{3,1,2,0:T(8,128)(2,1)} %copy.88), calls=%async_computation.1 | async-start | bytes 8388608 | tf_op jit(solution)/shard_map/all_to_all | solution.py:73
  34.9 178.1 %all-reduce.4.cloned.1.call-start = ((), (), s32[]{:S(2)}) async-start(), calls=%async_computation.3 | async-start | bytes 131072 | tf_op jit(solution)/shard_map/psum | solution.py:92
  35.0 45.5 %collective-permute-start.1 = (bf16[15,128]{1,0:T(8,128)(2,1)S(1)}, bf16[15,128]{1,0:T(8,128)(2,1)S(1)}, u32[]{:S(2)}, u32[]{:S(2)}) collective-permute-start(bf16[15,128]{1,0:T(8,128)(2,1)S(1)} %get-tuple-element.175), channel_id=1, source_target_pairs={{4,0},{8,4},{12,8},{5,1},{9,5},{13,9},{6,2},{10,6},{14,10},{7,3},{... | collective-permute-start | bytes 11528 | tf_op jit(solution)/shard_map/ppermute | solution.py:17
  36.3 64.5 %collective-permute-start = (bf16[15,128]{1,0:T(8,128)(2,1)S(1)}, bf16[15,128]{1,0:T(8,128)(2,1)S(1)}, u32[]{:S(2)}, u32[]{:S(2)}) collective-permute-start(bf16[15,128]{1,0:T(8,128)(2,1)S(1)} %get-tuple-element.174), channel_id=1, source_target_pairs={{0,4},{4,8},{8,12},{1,5},{5,9},{9,13},{2,6},{6,10},{10,14},{3,7},{... | collective-permute-start | bytes 11528 | tf_op jit(solution)/shard_map/ppermute | solution.py:14
  101.0 4.4 %collective-permute-start.3 = (bf16[286,15]{1,0:T(8,128)(2,1)S(1)}, bf16[286,15]{1,0:T(8,128)(2,1)S(1)}, u32[]{:S(2)}, u32[]{:S(2)}) collective-permute-start(bf16[286,15]{1,0:T(8,128)(2,1)S(1)} %get-tuple-element.171), channel_id=1, source_target_pairs={{2,0},{0,2},{3,1},{1,3},{6,4},{4,6},{7,5},{5,7},{10,8},{8,10},{11,... | collective-permute-start | bytes 25748 | tf_op jit(solution)/shard_map/ppermute | solution.py:17
  102.6 4.4 %collective-permute-start.2 = (bf16[286,15]{1,0:T(8,128)(2,1)S(1)}, bf16[286,15]{1,0:T(8,128)(2,1)S(1)}, u32[]{:S(2)}, u32[]{:S(2)}) collective-permute-start(bf16[286,15]{1,0:T(8,128)(2,1)S(1)} %get-tuple-element.170), channel_id=1, source_target_pairs={{0,2},{2,0},{1,3},{3,1},{4,6},{6,4},{5,7},{7,5},{8,10},{10,8},{9,1... | collective-permute-start | bytes 25748 | tf_op jit(solution)/shard_map/ppermute | solution.py:14
  145.0 10.4 %copy-start.1 = (f32[256,158]{1,0:T(8,128)S(1)}, f32[256,158]{1,0:T(8,128)}, u32[]{:S(2)}) copy-start(f32[256,158]{1,0:T(8,128)} %get-tuple-element.164) | copy-start | bytes 485380
  156.2 1.0 copy-start.2
  157.2 10.3 %copy-start.8 = (f32[4]{0:T(128)S(1)}, f32[4]{0:T(128)}, u32[]{:S(2)}) copy-start(f32[4]{0:T(128)} %get-tuple-element.92) | copy-start | bytes 52
  157.2 10.3 %copy-start.9 = (f32[4]{0:T(128)S(1)}, f32[4]{0:T(128)}, u32[]{:S(2)}) copy-start(f32[4]{0:T(128)} %get-tuple-element.93) | copy-start | bytes 52
  157.2 10.3 %copy-start.10 = (f32[4]{0:T(128)S(1)}, f32[4]{0:T(128)}, u32[]{:S(2)}) copy-start(f32[4]{0:T(128)} %get-tuple-element.94) | copy-start | bytes 52
  157.2 10.3 %copy-start.11 = (f32[4]{0:T(128)S(1)}, f32[4]{0:T(128)}, u32[]{:S(2)}) copy-start(f32[4]{0:T(128)} %get-tuple-element.95) | copy-start | bytes 52
  157.2 10.3 %copy-start.12 = (f32[4]{0:T(128)S(1)}, f32[4]{0:T(128)}, u32[]{:S(2)}) copy-start(f32[4]{0:T(128)} %get-tuple-element.96) | copy-start | bytes 52
  157.2 10.3 %copy-start.13 = (f32[4]{0:T(128)S(1)}, f32[4]{0:T(128)}, u32[]{:S(2)}) copy-start(f32[4]{0:T(128)} %get-tuple-element.97) | copy-start | bytes 52
  157.2 10.3 %copy-start.14 = (f32[4]{0:T(128)S(1)}, f32[4]{0:T(128)}, u32[]{:S(2)}) copy-start(f32[4]{0:T(128)} %get-tuple-element.67) | copy-start | bytes 52
  157.2 10.3 %copy-start.15 = (f32[4]{0:T(128)S(1)}, f32[4]{0:T(128)}, u32[]{:S(2)}) copy-start(f32[4]{0:T(128)} %get-tuple-element.68) | copy-start | bytes 52
  157.3 10.3 %copy-start.16 = (f32[4]{0:T(128)S(1)}, f32[4]{0:T(128)}, u32[]{:S(2)}) copy-start(f32[4]{0:T(128)} %get-tuple-element.69) | copy-start | bytes 52
  157.3 10.3 %copy-start.17 = (f32[4]{0:T(128)S(1)}, f32[4]{0:T(128)}, u32[]{:S(2)}) copy-start(f32[4]{0:T(128)} %get-tuple-element.70) | copy-start | bytes 52
  157.3 10.3 %copy-start.18 = (f32[4]{0:T(128)S(1)}, f32[4]{0:T(128)}, u32[]{:S(2)}) copy-start(f32[4]{0:T(128)} %get-tuple-element.71) | copy-start | bytes 52
  157.3 10.3 %copy-start.19 = (f32[4]{0:T(128)S(1)}, f32[4]{0:T(128)}, u32[]{:S(2)}) copy-start(f32[4]{0:T(128)} %get-tuple-element.72) | copy-start | bytes 52
  157.3 10.3 %copy-start.20 = (f32[4]{0:T(128)S(1)}, f32[4]{0:T(128)}, u32[]{:S(2)}) copy-start(f32[4]{0:T(128)} %get-tuple-element.73) | copy-start | bytes 52
  157.3 10.3 %copy-start.21 = (f32[4]{0:T(128)S(1)}, f32[4]{0:T(128)}, u32[]{:S(2)}) copy-start(f32[4]{0:T(128)} %get-tuple-element.74) | copy-start | bytes 52
  157.3 10.3 %copy-start.22 = (f32[4]{0:T(128)S(1)}, f32[4]{0:T(128)}, u32[]{:S(2)}) copy-start(f32[4]{0:T(128)} %get-tuple-element.75) | copy-start | bytes 52
  157.3 10.3 %copy-start.23 = (f32[4]{0:T(128)S(1)}, f32[4]{0:T(128)}, u32[]{:S(2)}) copy-start(f32[4]{0:T(128)} %get-tuple-element.76) | copy-start | bytes 52
  157.3 10.3 %copy-start.24 = (f32[4]{0:T(128)S(1)}, f32[4]{0:T(128)}, u32[]{:S(2)}) copy-start(f32[4]{0:T(128)} %get-tuple-element.77) | copy-start | bytes 52
  157.3 10.3 %copy-start.25 = (f32[4]{0:T(128)S(1)}, f32[4]{0:T(128)}, u32[]{:S(2)}) copy-start(f32[4]{0:T(128)} %get-tuple-element.78) | copy-start | bytes 52
  157.4 10.3 %copy-start.26 = (f32[4]{0:T(128)S(1)}, f32[4]{0:T(128)}, u32[]{:S(2)}) copy-start(f32[4]{0:T(128)} %get-tuple-element.79) | copy-start | bytes 52
  157.4 10.3 %copy-start.27 = (f32[4]{0:T(128)S(1)}, f32[4]{0:T(128)}, u32[]{:S(2)}) copy-start(f32[4]{0:T(128)} %get-tuple-element.80) | copy-start | bytes 52
  157.4 10.3 %copy-start.28 = (f32[4]{0:T(128)S(1)}, f32[4]{0:T(128)}, u32[]{:S(2)}) copy-start(f32[4]{0:T(128)} %get-tuple-element.81) | copy-start | bytes 52
  157.4 10.3 %copy-start.29 = (f32[4]{0:T(128)S(1)}, f32[4]{0:T(128)}, u32[]{:S(2)}) copy-start(f32[4]{0:T(128)} %get-tuple-element.82) | copy-start | bytes 52
  157.4 10.3 %copy-start.30 = (f32[4]{0:T(128)S(1)}, f32[4]{0:T(128)}, u32[]{:S(2)}) copy-start(f32[4]{0:T(128)} %get-tuple-element.83) | copy-start | bytes 52
  157.4 10.3 %copy-start.31 = (f32[4]{0:T(128)S(1)}, f32[4]{0:T(128)}, u32[]{:S(2)}) copy-start(f32[4]{0:T(128)} %get-tuple-element.84) | copy-start | bytes 52
  157.4 10.3 %copy-start.32 = (f32[4]{0:T(128)S(1)}, f32[4]{0:T(128)}, u32[]{:S(2)}) copy-start(f32[4]{0:T(128)} %get-tuple-element.85) | copy-start | bytes 52
  172.2 41.7 %copy-start.33 = (f32[256]{0:T(256)S(1)}, f32[256]{0:T(256)}, u32[]{:S(2)}) copy-start(f32[256]{0:T(256)} %broadcast_bitcast_fusion) | copy-start | bytes 3076
  172.2 120.9 %all-reduce.6.cloned.1.call-start = ((), (), s32[]{:S(2)}) async-start(), calls=%async_computation.4 | async-start | bytes 524288 | tf_op jit(solution)/shard_map/psum | solution.py:98
  214.5 16.0 %collective-permute-start.5 = (f32[2,4,15,128]{2,1,3,0:T(4,128)S(1)}, f32[2,4,15,128]{2,1,3,0:T(4,128)S(1)}, u32[]{:S(2)}, u32[]{:S(2)}) collective-permute-start(f32[2,4,15,128]{2,1,3,0:T(4,128)S(1)} %get-tuple-element.134), channel_id=1, source_target_pairs={{4,0},{8,4},{12,8},{5,1},{9,5},{13,9},{6,2},{10,6},{14,10},{7,3},{... | collective-permute-start | bytes 184328 | tf_op jit(solution)/shard_map/ppermute | solution.py:17
  215.8 15.9 %collective-permute-start.4 = (f32[2,4,15,128]{2,1,3,0:T(4,128)S(1)}, f32[2,4,15,128]{2,1,3,0:T(4,128)S(1)}, u32[]{:S(2)}, u32[]{:S(2)}) collective-permute-start(f32[2,4,15,128]{2,1,3,0:T(4,128)S(1)} %get-tuple-element.133), channel_id=1, source_target_pairs={{0,4},{4,8},{8,12},{1,5},{5,9},{9,13},{2,6},{6,10},{10,14},{3,7},{... | collective-permute-start | bytes 184328 | tf_op jit(solution)/shard_map/ppermute | solution.py:14
  232.0 7.6 %collective-permute-start.7 = (f32[2,4,286,15]{2,1,3,0:T(4,128)S(1)}, f32[2,4,286,15]{2,1,3,0:T(4,128)S(1)}, u32[]{:S(2)}, u32[]{:S(2)}) collective-permute-start(f32[2,4,286,15]{2,1,3,0:T(4,128)S(1)} %get-tuple-element.132), channel_id=1, source_target_pairs={{2,0},{0,2},{3,1},{1,3},{6,4},{4,6},{7,5},{5,7},{10,8},{8,10},{11,... | collective-permute-start | bytes 411848 | tf_op jit(solution)/shard_map/ppermute | solution.py:17
  233.8 8.0 %collective-permute-start.6 = (f32[2,4,286,15]{2,1,3,0:T(4,128)S(1)}, f32[2,4,286,15]{2,1,3,0:T(4,128)S(1)}, u32[]{:S(2)}, u32[]{:S(2)}) collective-permute-start(f32[2,4,286,15]{2,1,3,0:T(4,128)S(1)} %get-tuple-element.131), channel_id=1, source_target_pairs={{0,2},{2,0},{1,3},{3,1},{4,6},{6,4},{5,7},{7,5},{8,10},{10,8},{9,1... | collective-permute-start | bytes 411848 | tf_op jit(solution)/shard_map/ppermute | solution.py:14
  265.2 7.3 %copy-start.4 = (f32[256,128]{1,0:T(8,128)S(1)}, f32[256,128]{1,0:T(8,128)}, u32[]{:S(2)}) copy-start(f32[256,128]{1,0:T(8,128)} %param.8) | copy-start | bytes 393220
Sparse Core Ops, SparseCore 0:
  172.3 40.6 all-reduce.3
  272.6 20.4 all-reduce.5
where the time goes:
time: 303 us; the launch traced here: 302 us
  waiting for transfers between devices  138 us (46%)
  local copies, waits for them, and re-layouts  61.5 us (20%)
  other arithmetic  49.7 us (16%)
  starting transfers between devices  30.7 us (10%)
  between operations  14.1 us (5%)
  matrix products  7.66 us (3%)
    ppermute x4, waiting for transfers between devices, extended(): lax.ppermute(lax.slice_in_dim(block, 0, width, axis=dim), axis, backward)  49.9 us
    mul x31, local copies, waits for them, and re-layouts, sweep(): tap_stack[tap_index]  47.9 us
    psum x1, waiting for transfers between devices, body(): lax.psum(partial_value.astype(jnp.bfloat16), 'sub').astype(jnp.float32)  37.7 us
    add x2, other arithmetic, sweep(): running + tap_stack[tap_index] * lax.slice_in_dim(source, tap_index, tap_...  30.9 us
    ppermute x4, waiting for transfers between devices, extended(): lax.ppermute(lax.slice_in_dim(block, block.shape[dim] - width, None, axis...  25.1 us
    psum x1, waiting for transfers between devices, body(): numerator, denominator = lax.psum((backward[0], backward[1]), 'sub')  20.5 us
    ppermute x4, starting transfers between devices, extended(): lax.ppermute(lax.slice_in_dim(block, block.shape[dim] - width, None, axis...  10.4 us
    reduce_sum x1, other arithmetic, body(): jnp.sum(separable(weighted, row_behind, col_behind, tile_rows, block_size...  6.54 us
  transfers between devices with their start and end apart: 13, of which 12 were waited for; matrix products, arithmetic and copies ran while one was open for 27% of the time, Pallas kernels for 0%

commit v1 on v0

--- a/solution.py
+++ b/solution.py
@@ -89,7 +89,9 @@
     partial_value = jnp.sum(
         weight_stack * separable(padded[None], row_ahead, col_ahead, tile_rows, block_size), axis=0
     )
-    smeared_image = lax.psum(partial_value.astype(jnp.bfloat16), "sub").astype(jnp.float32)
+    smeared_image = jnp.sum(
+        lax.all_gather(partial_value.astype(jnp.bfloat16), "sub"), axis=0
+    ).astype(jnp.float32)
     quotient = counts / smeared_image
     stacked = jnp.stack([weight_stack * quotient[None], weight_stack * coverage[None]])
     weighted = extended(stacked, (("tube", 2),), margin, False)

time: 303 us -> 288 us (0.950)
  waiting for transfers between devices: 138 us -> 98.9 us
  starting transfers between devices: 30.7 us -> 54.7 us
    psum x1 -> x0, waiting for transfers between devices: 37.7 us -> none  [body(): lax.psum(partial_value.astype(jnp.bfloat16), 'sub').astype(jnp.float32)]
    ppermute x4, starting transfers between devices: 10.4 us -> 35.3 us  [extended(): lax.ppermute(lax.slice_in_dim(block, block.shape[dim] - width, None, axis...]
  transfers between devices with their start and end apart: 13 -> 12, of which waited for: 12 -> 11; matrix products, arithmetic and copies ran while one was open for 27% -> 27% of each run, Pallas kernels for 0% -> 0%
where the time goes in v1:
time: 288 us; the launch traced here: 287 us
  waiting for transfers between devices  98.9 us (34%)
  local copies, waits for them, and re-layouts  61.3 us (21%)
  starting transfers between devices  54.7 us (19%)
  other arithmetic  48.5 us (17%)
  between operations  14.1 us (5%)
  matrix products  7.66 us (3%)
    ppermute x4, waiting for transfers between devices, extended(): lax.ppermute(lax.slice_in_dim(block, 0, width, axis=dim), axis, backward)  50.1 us
    mul x31, local copies, waits for them, and re-layouts, sweep(): tap_stack[tap_index]  47.8 us
    ppermute x4, starting transfers between devices, extended(): lax.ppermute(lax.slice_in_dim(block, block.shape[dim] - width, None, axis...  35.3 us
    add x2, other arithmetic, sweep(): running + tap_stack[tap_index] * lax.slice_in_dim(source, tap_index, tap_...  30.9 us
    ppermute x4, waiting for transfers between devices, extended(): lax.ppermute(lax.slice_in_dim(block, block.shape[dim] - width, None, axis...  25.2 us
    psum x1, waiting for transfers between devices, body(): numerator, denominator = lax.psum((backward[0], backward[1]), 'sub')  18.7 us
    reduce_sum x1, other arithmetic, body(): jnp.sum(separable(weighted, row_behind, col_behind, tile_rows, block_size...  6.54 us
    all_to_all x1, starting transfers between devices, body(): lax.all_to_all(send_places, 'tube', split_axis=0, concat_axis=0, tiled=True)  6.32 us
  transfers between devices with their start and end apart: 12, of which 11 were waited for; matrix products, arithmetic and copies ran while one was open for 27% of the time, Pallas kernels for 0%

profile of v1, /device:TPU:0, one launch (start us, length us, event | category | flops | bytes accessed | tf_op | source)
XLA Modules:
  0.0 287.1 jit_solution(4810684406019213218)
XLA Ops:
  9.6 6.3 %all-to-all-start = ((bf16[4,32,2]{1,2,0:T(2,128)(2,1)}), bf16[4,32,2]{1,2,0:T(2,128)(2,1)S(1)}, u32[]{:S(2)}, u32[]{:S(2)}) async-start(bf16[4,32,2]{1,2,0:T(2,128)(2,1)} %convolution_convert_fusion.2), calls=%async_computation | async-start | bytes 4096 | tf_op jit(solution)/shard_map/all_to_all | solution.py:74
  17.3 4.1 %all-to-all-done = bf16[4,32,2]{1,2,0:T(2,128)(2,1)S(1)} async-done(((bf16[4,32,2]{1,2,0:T(2,128)(2,1)}), bf16[4,32,2]{1,2,0:T(2,128)(2,1)S(1)}, u32[]{:S(2)}, u32[]{:S(2)}) %all-to-all-start) | async-done | bytes 544 | tf_op jit(solution)/shard_map/all_to_all | solution.py:74
  21.4 3.2 %all-to-all-start.2 = ((bf16[4,32,2]{1,2,0:T(2,128)(2,1)}), bf16[4,32,2]{1,2,0:T(2,128)(2,1)S(1)}, u32[]{:S(2)}, u32[]{:S(2)}) async-start(bf16[4,32,2]{1,2,0:T(2,128)(2,1)} %convolution_convert_fusion.1), calls=%async_computation.2 | async-start | bytes 4096 | tf_op jit(solution)/shard_map/all_to_all | solution.py:75
  24.6 1.9 convolution_convert_fusion
  26.5 2.7 copy.127
  30.1 4.8 %all-to-all-start.1 = ((bf16[4,32,128,128]{3,1,2,0:T(8,128)(2,1)}), bf16[4,32,128,128]{3,1,2,0:T(8,128)(2,1)}, u32[]{:S(2)}, u32[]{:S(2)}) async-start(bf16[4,32,128,128]{3,1,2,0:T(8,128)(2,1)} %copy.127), calls=%async_computation.1 | async-start | bytes 8388608 | tf_op jit(solution)/shard_map/all_to_all | solution.py:73
  36.3 4.7 %collective-permute-start = (bf16[15,128]{1,0:T(8,128)(2,1)S(1)}, bf16[15,128]{1,0:T(8,128)(2,1)S(1)}, u32[]{:S(2)}, u32[]{:S(2)}) collective-permute-start(bf16[15,128]{1,0:T(8,128)(2,1)S(1)} %get-tuple-element.174), channel_id=1, source_target_pairs={{0,4},{4,8},{8,12},{1,5},{5,9},{9,13},{2,6},{6,10},{10,14},{3,7},{... | collective-permute-start | bytes 11528 | tf_op jit(solution)/shard_map/ppermute | solution.py:14
  46.5 34.0 %collective-permute-done.1 = bf16[15,128]{1,0:T(8,128)(2,1)S(1)} collective-permute-done((bf16[15,128]{1,0:T(8,128)(2,1)S(1)}, bf16[15,128]{1,0:T(8,128)(2,1)S(1)}, u32[]{:S(2)}, u32[]{:S(2)}) %collective-permute-start.1) | collective-permute-done | bytes 3872 | tf_op jit(solution)/shard_map/ppermute | solution.py:17
  80.6 20.3 %collective-permute-done = bf16[15,128]{1,0:T(8,128)(2,1)S(1)} collective-permute-done((bf16[15,128]{1,0:T(8,128)(2,1)S(1)}, bf16[15,128]{1,0:T(8,128)(2,1)S(1)}, u32[]{:S(2)}, u32[]{:S(2)}) %collective-permute-start) | collective-permute-done | bytes 3872 | tf_op jit(solution)/shard_map/ppermute | solution.py:14
  103.7 1.7 collective-permute-done.3
  107.0 2.1 slice_bitcast_fusion.30
  109.1 1.7 copy.160
  110.9 1.7 copy.159
  112.6 1.7 copy.158
  114.3 1.7 copy.157
  116.0 1.7 copy.156
  117.8 1.7 copy.155
  119.5 1.7 copy.154
  121.2 1.7 copy.153
  122.9 1.7 copy.152
  124.7 1.7 copy.151
  126.4 1.7 copy.150
  128.1 1.7 copy.149
  129.8 1.7 copy.148
  131.5 1.7 copy.147
  133.2 1.7 copy.146
  135.0 1.7 copy.145
  139.8 1.7 copy.142
  141.5 1.7 copy.141
  143.2 1.7 copy.140
  144.9 1.8 copy.139
  146.7 1.7 copy.138
  148.4 1.7 copy.137
  150.2 1.7 copy.136
  151.9 1.7 copy.135
  153.6 1.7 copy.134
  157.3 10.0 %multiply_add_fusion = f32[4,256,158]{1,0,2:T(4,128)S(1)} fusion(f32[256,158]{0,1:T(8,128)S(1)} %copy-done.2, f32[4]{0:T(128)} %get-tuple-element.99, f32[256,158]{0,1:T(8,128)} %copy.159, f32[4]{0:T(128)} %get-tuple-element.100, f32[256,158]{0,1:T(8,128)} %copy.158, f32[4]{0:T(128)} %get-tuple-element.101, f32[256,158]{0,1:T(8,128)} %copy.157, ...), kind=kLoop, calls=%fused_computation.134 | loop fusion | flops 9869312 | bytes 5663216 | tf_op jit(solution)/shard_map/add | solution.py:25
  167.6 3.8 %fusion.62 = bf16[256,128]{0,1:T(8,128)(2,1)S(1)} fusion(bf16[4,256,128]{1,0,2:T(4,128)(2,1)S(1)} %copy.125, f32[4,256,158]{1,0,2:T(4,128)S(1)} %multiply_add_fusion, f32[4]{0:T(128)S(1)} %copy-done.15, f32[4]{0:T(128)S(1)} %copy-done.16, f32[4]{0:T(128)S(1)} %copy-done.17, f32[4]{0:T(128)S(1)} %copy-done.18, f32[4]{0:T(128)S(1)} %copy-done.19, ...), kind=kLoop, calls=%fused_computation.135 | loop fusion | flops 8355840 | bytes 16581104 | tf_op jit(solution)/shard_map/reduce_sum | solution.py:89
  171.5 1.9 all-gather
  173.8 2.9 %convolution_bitcast_fusion = f32[2,128,128]{2,0,1:T(2,128)S(1)} fusion(bf16[4,32,128,128]{3,1,2,0:T(8,128)(2,1)} %all-to-all-done.1, bf16[4,32,2]{1,2,0:T(2,128)(2,1)S(1)} %all-to-all-done), kind=kOutput, calls=%fused_computation.64 | convolution fusion | flops 8388608 | bytes 4325888 | tf_op jit(solution)/shard_map/tcr,tcxy->rxy/dot_general | solution.py:77
  178.7 28.8 %collective-permute-start.4 = (f32[2,4,15,128]{2,1,3,0:T(4,128)S(1)}, f32[2,4,15,128]{2,1,3,0:T(4,128)S(1)}, u32[]{:S(2)}, u32[]{:S(2)}) collective-permute-start(f32[2,4,15,128]{2,1,3,0:T(4,128)S(1)} %get-tuple-element.133), channel_id=1, source_target_pairs={{0,4},{4,8},{8,12},{1,5},{5,9},{9,13},{2,6},{6,10},{10,14},{3,7},{... | collective-permute-start | bytes 184328 | tf_op jit(solution)/shard_map/ppermute | solution.py:14
  207.9 9.7 %collective-permute-done.5 = f32[2,4,15,128]{2,1,3,0:T(4,128)S(1)} collective-permute-done((f32[2,4,15,128]{2,1,3,0:T(4,128)S(1)}, f32[2,4,15,128]{2,1,3,0:T(4,128)S(1)}, u32[]{:S(2)}, u32[]{:S(2)}) %collective-permute-start.5) | collective-permute-done | bytes 61472 | tf_op jit(solution)/shard_map/ppermute | solution.py:17
  222.0 4.7 %collective-permute-done.7 = f32[2,4,286,15]{2,1,3,0:T(4,128)S(1)} collective-permute-done((f32[2,4,286,15]{2,1,3,0:T(4,128)S(1)}, f32[2,4,286,15]{2,1,3,0:T(4,128)S(1)}, u32[]{:S(2)}, u32[]{:S(2)}) %collective-permute-start.7) | collective-permute-done | bytes 137312 | tf_op jit(solution)/shard_map/ppermute | solution.py:17
  226.7 2.2 collective-permute-done.6
  229.0 2.6 pad_maximum_fusion
  231.5 20.9 %fusion.1 = f32[2,4,256,158]{2,1,3,0:T(4,128)S(1)} fusion(f32[2,4,286,158]{2,1,3,0:T(4,128)S(1)} %pad_maximum_fusion, f32[4]{0:T(128)S(1)} %get-tuple-element.37, f32[4]{0:T(128)S(1)} %get-tuple-element.38, f32[4]{0:T(128)S(1)} %get-tuple-element.39, f32[4]{0:T(128)S(1)} %get-tuple-element.40, f32[4]{0:T(128)S(1)} %get-tuple-element.41, ...), kind=kLoop, calls=%fused_computation.4 | loop fusion | flops 19738624 | bytes 41419248 | tf_op jit(solution)/shard_map/add | solution.py:25
  252.4 6.5 %fusion.32 = f32[2,256,128]{1,2,0:T(8,128)S(1)} fusion(f32[2,4,256,158]{2,1,3,0:T(4,128)S(1)} %fusion.1, f32[4]{0:T(128)S(1)} %get-tuple-element.6, f32[4]{0:T(128)S(1)} %get-tuple-element.7, f32[4]{0:T(128)S(1)} %get-tuple-element.8, f32[4]{0:T(128)S(1)} %get-tuple-element.9, f32[4]{0:T(128)S(1)} %get-tuple-element.10, f32[4]{0:T(128)S(1)} %get-tuple-element.11, ...), kind=kLoop, calls=%fused_computation.69 | loop fusion | flops 16187392 | bytes 32768496 | tf_op jit(solution)/shard_map/reduce_sum | solution.py:99
  259.8 18.7 %all-reduce.3.cloned.1.call-done = (f32[256,128]{0,1:T(8,128)}, f32[256,128]{0,1:T(8,128)}) async-done(((f32[256,128]{0,1:T(8,128)}, f32[256,128]{0,1:T(8,128)}), (f32[256,128]{0,1:T(8,128)}, f32[256,128]{0,1:T(8,128)})) %all-reduce.3.cloned.1.call-update) | async-done | bytes 262160 | tf_op jit(solution)/shard_map/psum | solution.py:100
  (128 shorter events, 31.2 us)
Async XLA Ops:
  6.5 18.1 %copy-start = (bf16[1,64,128,128]{3,2,1,0:T(8,128)(2,1)S(1)}, bf16[1,64,128,128]{3,2,1,0:T(8,128)(2,1)}, u32[]{:S(2)}) copy-start(bf16[1,64,128,128]{3,2,1,0:T(8,128)(2,1)} %param.12) | copy-start | bytes 6291460
  9.6 11.8 %all-to-all-start = ((bf16[4,32,2]{1,2,0:T(2,128)(2,1)}), bf16[4,32,2]{1,2,0:T(2,128)(2,1)S(1)}, u32[]{:S(2)}, u32[]{:S(2)}) async-start(bf16[4,32,2]{1,2,0:T(2,128)(2,1)} %convolution_convert_fusion.2), calls=%async_computation | async-start | bytes 4096 | tf_op jit(solution)/shard_map/all_to_all | solution.py:74
  21.4 8.7 %all-to-all-start.2 = ((bf16[4,32,2]{1,2,0:T(2,128)(2,1)}), bf16[4,32,2]{1,2,0:T(2,128)(2,1)S(1)}, u32[]{:S(2)}, u32[]{:S(2)}) async-start(bf16[4,32,2]{1,2,0:T(2,128)(2,1)} %convolution_convert_fusion.1), calls=%async_computation.2 | async-start | bytes 4096 | tf_op jit(solution)/shard_map/all_to_all | solution.py:75
  29.3 5.7 %copy-start.3 = (f32[256,128]{1,0:T(8,128)S(1)}, f32[256,128]{1,0:T(8,128)}, u32[]{:S(2)}) copy-start(f32[256,128]{1,0:T(8,128)} %param.8) | copy-start | bytes 393220
  29.3 11.8 %copy-start.5 = (bf16[4,256,128]{2,1,0:T(8,128)(2,1)S(1)}, bf16[4,256,128]{2,1,0:T(8,128)(2,1)}, u32[]{:S(2)}) copy-start(bf16[4,256,128]{2,1,0:T(8,128)(2,1)} %param.9) | copy-start | bytes 786436
  29.3 12.0 %copy-start.6 = (f32[4,31]{1,0:T(4,128)S(1)}, f32[4,31]{1,0:T(4,128)}, u32[]{:S(2)}) copy-start(f32[4,31]{1,0:T(4,128)} %param.10) | copy-start | bytes 1492
  29.3 12.1 %copy-start.7 = (f32[4,31]{1,0:T(4,128)S(1)}, f32[4,31]{1,0:T(4,128)}, u32[]{:S(2)}) copy-start(f32[4,31]{1,0:T(4,128)} %param.11) | copy-start | bytes 1492
  30.1 143.7 %all-to-all-start.1 = ((bf16[4,32,128,128]{3,1,2,0:T(8,128)(2,1)}), bf16[4,32,128,128]{3,1,2,0:T(8,128)(2,1)}, u32[]{:S(2)}, u32[]{:S(2)}) async-start(bf16[4,32,128,128]{3,1,2,0:T(8,128)(2,1)} %copy.127), calls=%async_computation.1 | async-start | bytes 8388608 | tf_op jit(solution)/shard_map/all_to_all | solution.py:73
  34.9 243.5 %all-reduce.3.cloned.1.call-start = ((), (), s32[]{:S(2)}) async-start(), calls=%async_computation.3 | async-start | bytes 524288 | tf_op jit(solution)/shard_map/psum | solution.py:100
  35.0 45.5 %collective-permute-start.1 = (bf16[15,128]{1,0:T(8,128)(2,1)S(1)}, bf16[15,128]{1,0:T(8,128)(2,1)S(1)}, u32[]{:S(2)}, u32[]{:S(2)}) collective-permute-start(bf16[15,128]{1,0:T(8,128)(2,1)S(1)} %get-tuple-element.175), channel_id=1, source_target_pairs={{4,0},{8,4},{12,8},{5,1},{9,5},{13,9},{6,2},{10,6},{14,10},{7,3},{... | collective-permute-start | bytes 11528 | tf_op jit(solution)/shard_map/ppermute | solution.py:17
  36.3 64.5 %collective-permute-start = (bf16[15,128]{1,0:T(8,128)(2,1)S(1)}, bf16[15,128]{1,0:T(8,128)(2,1)S(1)}, u32[]{:S(2)}, u32[]{:S(2)}) collective-permute-start(bf16[15,128]{1,0:T(8,128)(2,1)S(1)} %get-tuple-element.174), channel_id=1, source_target_pairs={{0,4},{4,8},{8,12},{1,5},{5,9},{9,13},{2,6},{6,10},{10,14},{3,7},{... | collective-permute-start | bytes 11528 | tf_op jit(solution)/shard_map/ppermute | solution.py:14
  101.0 4.4 %collective-permute-start.3 = (bf16[286,15]{1,0:T(8,128)(2,1)S(1)}, bf16[286,15]{1,0:T(8,128)(2,1)S(1)}, u32[]{:S(2)}, u32[]{:S(2)}) collective-permute-start(bf16[286,15]{1,0:T(8,128)(2,1)S(1)} %get-tuple-element.171), channel_id=1, source_target_pairs={{2,0},{0,2},{3,1},{1,3},{6,4},{4,6},{7,5},{5,7},{10,8},{8,10},{11,... | collective-permute-start | bytes 25748 | tf_op jit(solution)/shard_map/ppermute | solution.py:17
  102.6 4.4 %collective-permute-start.2 = (bf16[286,15]{1,0:T(8,128)(2,1)S(1)}, bf16[286,15]{1,0:T(8,128)(2,1)S(1)}, u32[]{:S(2)}, u32[]{:S(2)}) collective-permute-start(bf16[286,15]{1,0:T(8,128)(2,1)S(1)} %get-tuple-element.170), channel_id=1, source_target_pairs={{0,2},{2,0},{1,3},{3,1},{4,6},{6,4},{5,7},{7,5},{8,10},{10,8},{9,1... | collective-permute-start | bytes 25748 | tf_op jit(solution)/shard_map/ppermute | solution.py:14
  144.9 10.4 %copy-start.1 = (f32[256,158]{1,0:T(8,128)S(1)}, f32[256,158]{1,0:T(8,128)}, u32[]{:S(2)}) copy-start(f32[256,158]{1,0:T(8,128)} %get-tuple-element.164) | copy-start | bytes 485380
  156.1 1.0 copy-start.2
  157.1 10.3 %copy-start.8 = (f32[4]{0:T(128)S(1)}, f32[4]{0:T(128)}, u32[]{:S(2)}) copy-start(f32[4]{0:T(128)} %get-tuple-element.92) | copy-start | bytes 52
  157.1 10.3 %copy-start.9 = (f32[4]{0:T(128)S(1)}, f32[4]{0:T(128)}, u32[]{:S(2)}) copy-start(f32[4]{0:T(128)} %get-tuple-element.93) | copy-start | bytes 52
  157.1 10.3 %copy-start.10 = (f32[4]{0:T(128)S(1)}, f32[4]{0:T(128)}, u32[]{:S(2)}) copy-start(f32[4]{0:T(128)} %get-tuple-element.94) | copy-start | bytes 52
  157.1 10.3 %copy-start.11 = (f32[4]{0:T(128)S(1)}, f32[4]{0:T(128)}, u32[]{:S(2)}) copy-start(f32[4]{0:T(128)} %get-tuple-element.95) | copy-start | bytes 52
  157.1 10.3 %copy-start.12 = (f32[4]{0:T(128)S(1)}, f32[4]{0:T(128)}, u32[]{:S(2)}) copy-start(f32[4]{0:T(128)} %get-tuple-element.96) | copy-start | bytes 52
  157.1 10.3 %copy-start.13 = (f32[4]{0:T(128)S(1)}, f32[4]{0:T(128)}, u32[]{:S(2)}) copy-start(f32[4]{0:T(128)} %get-tuple-element.97) | copy-start | bytes 52
  157.2 10.3 %copy-start.14 = (f32[4]{0:T(128)S(1)}, f32[4]{0:T(128)}, u32[]{:S(2)}) copy-start(f32[4]{0:T(128)} %get-tuple-element.67) | copy-start | bytes 52
  157.2 10.3 %copy-start.15 = (f32[4]{0:T(128)S(1)}, f32[4]{0:T(128)}, u32[]{:S(2)}) copy-start(f32[4]{0:T(128)} %get-tuple-element.68) | copy-start | bytes 52
  157.2 10.3 %copy-start.16 = (f32[4]{0:T(128)S(1)}, f32[4]{0:T(128)}, u32[]{:S(2)}) copy-start(f32[4]{0:T(128)} %get-tuple-element.69) | copy-start | bytes 52
  157.2 10.3 %copy-start.17 = (f32[4]{0:T(128)S(1)}, f32[4]{0:T(128)}, u32[]{:S(2)}) copy-start(f32[4]{0:T(128)} %get-tuple-element.70) | copy-start | bytes 52
  157.2 10.3 %copy-start.18 = (f32[4]{0:T(128)S(1)}, f32[4]{0:T(128)}, u32[]{:S(2)}) copy-start(f32[4]{0:T(128)} %get-tuple-element.71) | copy-start | bytes 52
  157.2 10.3 %copy-start.19 = (f32[4]{0:T(128)S(1)}, f32[4]{0:T(128)}, u32[]{:S(2)}) copy-start(f32[4]{0:T(128)} %get-tuple-element.72) | copy-start | bytes 52
  157.2 10.3 %copy-start.20 = (f32[4]{0:T(128)S(1)}, f32[4]{0:T(128)}, u32[]{:S(2)}) copy-start(f32[4]{0:T(128)} %get-tuple-element.73) | copy-start | bytes 52
  157.2 10.3 %copy-start.21 = (f32[4]{0:T(128)S(1)}, f32[4]{0:T(128)}, u32[]{:S(2)}) copy-start(f32[4]{0:T(128)} %get-tuple-element.74) | copy-start | bytes 52
  157.2 10.3 %copy-start.22 = (f32[4]{0:T(128)S(1)}, f32[4]{0:T(128)}, u32[]{:S(2)}) copy-start(f32[4]{0:T(128)} %get-tuple-element.75) | copy-start | bytes 52
  157.2 10.3 %copy-start.23 = (f32[4]{0:T(128)S(1)}, f32[4]{0:T(128)}, u32[]{:S(2)}) copy-start(f32[4]{0:T(128)} %get-tuple-element.76) | copy-start | bytes 52
  157.3 10.3 %copy-start.24 = (f32[4]{0:T(128)S(1)}, f32[4]{0:T(128)}, u32[]{:S(2)}) copy-start(f32[4]{0:T(128)} %get-tuple-element.77) | copy-start | bytes 52
  157.3 10.3 %copy-start.25 = (f32[4]{0:T(128)S(1)}, f32[4]{0:T(128)}, u32[]{:S(2)}) copy-start(f32[4]{0:T(128)} %get-tuple-element.78) | copy-start | bytes 52
  157.3 10.3 %copy-start.26 = (f32[4]{0:T(128)S(1)}, f32[4]{0:T(128)}, u32[]{:S(2)}) copy-start(f32[4]{0:T(128)} %get-tuple-element.79) | copy-start | bytes 52
  157.3 10.3 %copy-start.27 = (f32[4]{0:T(128)S(1)}, f32[4]{0:T(128)}, u32[]{:S(2)}) copy-start(f32[4]{0:T(128)} %get-tuple-element.80) | copy-start | bytes 52
  157.3 10.3 %copy-start.28 = (f32[4]{0:T(128)S(1)}, f32[4]{0:T(128)}, u32[]{:S(2)}) copy-start(f32[4]{0:T(128)} %get-tuple-element.81) | copy-start | bytes 52
  157.3 10.3 %copy-start.29 = (f32[4]{0:T(128)S(1)}, f32[4]{0:T(128)}, u32[]{:S(2)}) copy-start(f32[4]{0:T(128)} %get-tuple-element.82) | copy-start | bytes 52
  157.3 10.3 %copy-start.30 = (f32[4]{0:T(128)S(1)}, f32[4]{0:T(128)}, u32[]{:S(2)}) copy-start(f32[4]{0:T(128)} %get-tuple-element.83) | copy-start | bytes 52
  157.3 10.3 %copy-start.31 = (f32[4]{0:T(128)S(1)}, f32[4]{0:T(128)}, u32[]{:S(2)}) copy-start(f32[4]{0:T(128)} %get-tuple-element.84) | copy-start | bytes 52
  157.3 10.3 %copy-start.32 = (f32[4]{0:T(128)S(1)}, f32[4]{0:T(128)}, u32[]{:S(2)}) copy-start(f32[4]{0:T(128)} %get-tuple-element.85) | copy-start | bytes 52
  173.7 3.1 %copy-start.33 = (f32[256]{0:T(256)S(1)}, f32[256]{0:T(256)}, u32[]{:S(2)}) copy-start(f32[256]{0:T(256)} %broadcast_bitcast_fusion) | copy-start | bytes 3076
  177.4 40.2 %collective-permute-start.5 = (f32[2,4,15,128]{2,1,3,0:T(4,128)S(1)}, f32[2,4,15,128]{2,1,3,0:T(4,128)S(1)}, u32[]{:S(2)}, u32[]{:S(2)}) collective-permute-start(f32[2,4,15,128]{2,1,3,0:T(4,128)S(1)} %get-tuple-element.134), channel_id=1, source_target_pairs={{4,0},{8,4},{12,8},{5,1},{9,5},{13,9},{6,2},{10,6},{14,10},{7,3},{... | collective-permute-start | bytes 184328 | tf_op jit(solution)/shard_map/ppermute | solution.py:17
  178.7 40.0 %collective-permute-start.4 = (f32[2,4,15,128]{2,1,3,0:T(4,128)S(1)}, f32[2,4,15,128]{2,1,3,0:T(4,128)S(1)}, u32[]{:S(2)}, u32[]{:S(2)}) collective-permute-start(f32[2,4,15,128]{2,1,3,0:T(4,128)S(1)} %get-tuple-element.133), channel_id=1, source_target_pairs={{0,4},{4,8},{8,12},{1,5},{5,9},{9,13},{2,6},{6,10},{10,14},{3,7},{... | collective-permute-start | bytes 184328 | tf_op jit(solution)/shard_map/ppermute | solution.py:14
  219.1 7.6 %collective-permute-start.7 = (f32[2,4,286,15]{2,1,3,0:T(4,128)S(1)}, f32[2,4,286,15]{2,1,3,0:T(4,128)S(1)}, u32[]{:S(2)}, u32[]{:S(2)}) collective-permute-start(f32[2,4,286,15]{2,1,3,0:T(4,128)S(1)} %get-tuple-element.132), channel_id=1, source_target_pairs={{2,0},{0,2},{3,1},{1,3},{6,4},{4,6},{7,5},{5,7},{10,8},{8,10},{11,... | collective-permute-start | bytes 411848 | tf_op jit(solution)/shard_map/ppermute | solution.py:17
  219.9 9.0 %collective-permute-start.6 = (f32[2,4,286,15]{2,1,3,0:T(4,128)S(1)}, f32[2,4,286,15]{2,1,3,0:T(4,128)S(1)}, u32[]{:S(2)}, u32[]{:S(2)}) collective-permute-start(f32[2,4,286,15]{2,1,3,0:T(4,128)S(1)} %get-tuple-element.131), channel_id=1, source_target_pairs={{0,2},{2,0},{1,3},{3,1},{4,6},{6,4},{5,7},{7,5},{8,10},{10,8},{9,1... | collective-permute-start | bytes 411848 | tf_op jit(solution)/shard_map/ppermute | solution.py:14
  252.4 7.3 %copy-start.4 = (f32[256,128]{1,0:T(8,128)S(1)}, f32[256,128]{1,0:T(8,128)}, u32[]{:S(2)}) copy-start(f32[256,128]{1,0:T(8,128)} %param.8) | copy-start | bytes 393220
Sparse Core Ops, SparseCore 0:
  259.8 18.6 all-reduce.2
